TPU v7x, 512 devices: a whole 4x8x8 slice. The times are simulated.
512 devices in a mesh: blk: 128 (over x, z_lo, y, core), rows: 4 (over z_hi).
Axes of the slice: x: 4, y: 8, z: 8 (z_hi: 4, z_lo: 2; z = z_hi * 2 + z_lo), core: 2. Of those that a mesh axis runs over, the one named last changes fastest.
Arguments:
- weight: bfloat16 [1024, 16384], P('blk', 'rows')
- factor: bfloat16 [16384, 16384], P('rows', 'blk')
- pairing: int32 [4, 64], replicated, may hold values from 0 to 63, each once within a row
Outputs:
- rotated: float32 [1024, 16384], P('rows', 'blk')
- right_factor: float32 [16384, 16384], P('rows', 'blk')
Inputs may be any that keep to these rules, and one draw needn't show every extreme that they name: Each row of pairing lists every column index of a block once.
All inputs are finite; a program needn't handle non-finite values.
Results may differ from a plain program's by a relative error of at most 0.0003.
Values may be sent and summed in bfloat16 or wider, within the bound.
A program may use at most 64 MiB of HBM per device.

v0:
```python
import jax
import jax.numpy as jnp
from jax import lax
from jax.sharding import PartitionSpec as P

BLOCK = 64
STEPS = 4


def shifted(x, axis, by):
    count = lax.axis_size(axis)
    return lax.ppermute(x, axis, [(i, (i + by) % count) for i in range(count)])


def turn_pair(upper_cols, lower_cols, upper_factor, lower_factor, pair_order):
    columns = pair_order.shape[0]
    ladder = lax.broadcasted_iota(jnp.int32, (columns, columns), 0)
    targets = lax.broadcasted_iota(jnp.int32, (columns, columns), 1)
    matches = (pair_order[:, None] == targets).astype(jnp.int32)
    inverse = jnp.sum(matches * ladder, axis=0)
    partner = jnp.take(lower_cols, pair_order, axis=0)
    partner_factor = jnp.take(lower_factor, pair_order, axis=0)
    upper_norm = jnp.sum(upper_cols * upper_cols, axis=1)
    lower_norm = jnp.sum(partner * partner, axis=1)
    cross_term = jnp.sum(upper_cols * partner, axis=1)
    upper_norm, lower_norm, cross_term = lax.psum((upper_norm, lower_norm, cross_term), "rows")
    rotation_angle = 0.5 * jnp.arctan2(2.0 * cross_term, upper_norm - lower_norm)
    cosine = jnp.cos(rotation_angle)[:, None]
    sine_part = jnp.sin(rotation_angle)[:, None]
    new_upper = cosine * upper_cols + sine_part * partner
    new_partner = cosine * partner - sine_part * upper_cols
    new_upper_factor = cosine * upper_factor + sine_part * partner_factor
    new_partner_factor = cosine * partner_factor - sine_part * upper_factor
    return (
        new_upper,
        jnp.take(new_partner, inverse, axis=0),
        new_upper_factor,
        jnp.take(new_partner_factor, inverse, axis=0),
    )


def per_device(weight, factor, pairing):
    partial_cols = lax.dot_general(
        factor,
        lax.all_gather(weight, "blk", axis=0, tiled=True),
        (((0,), (1,)), ((), ())),
        preferred_element_type=jnp.float32,
    )
    whitened = lax.psum_scatter(partial_cols, "rows", scatter_dimension=1, tiled=True)
    upper_cols = whitened[:BLOCK, :]
    lower_cols = whitened[BLOCK:, :]
    right_cols = factor.astype(jnp.float32).T
    upper_factor = right_cols[:BLOCK, :]
    lower_factor = right_cols[BLOCK:, :]
    for step_index in range(STEPS):
        if step_index > 0:
            upper_cols, upper_factor = shifted((upper_cols, upper_factor), "blk", 1)
            lower_cols, lower_factor = shifted((lower_cols, lower_factor), "blk", -1)
        upper_cols, lower_cols, upper_factor, lower_factor = turn_pair(
            upper_cols, lower_cols, upper_factor, lower_factor, pairing[step_index]
        )
    rotated = jnp.concatenate([upper_cols, lower_cols], axis=0)
    right_factor = jnp.concatenate([upper_factor, lower_factor], axis=0)
    return (rotated.T, right_factor.T)


def solution(mesh):
    in_specs = (P("blk", "rows"), P("rows", "blk"), P())
    out_specs = (P("rows", "blk"), P("rows", "blk"))
    return jax.shard_map(
        per_device, mesh=mesh, in_specs=in_specs, out_specs=out_specs, check_vma=False
    )
```

profile of v0, /device:TPU:128, one launch (start us, length us, event | category | flops | bytes accessed | tf_op | source)
XLA Modules:
  0.0 416.7 jit_solution(13958710799210260204)
XLA Ops:
  8.0 2.3 copy.8
  12.0 223.4 %all-gather.2.cloned.1.call-done = bf16[1024,4096]{1,0:T(8,128)(2,1)} async-done(((bf16[8,4096]{1,0:T(8,128)(2,1)}), bf16[1024,4096]{1,0:T(8,128)(2,1)}) %all-gather.2.cloned.1.call-update) | async-done | bytes 8388624 | tf_op jit(solution)/shard_map/all_gather | solution.py:45
  235.5 7.1 %fusion.4 = f32[128,1024]{1,0:T(8,128)} fusion(bf16[4096,128]{1,0:T(8,128)(2,1)S(1)} %copy-done, bf16[1024,4096]{1,0:T(8,128)(2,1)} %all-gather.2.cloned.1.call-done), kind=kOutput, calls=%fused_computation.99 | convolution fusion | flops 1073741824 | bytes 9961472 | tf_op jit(solution)/shard_map/dot_general | solution.py:43
  244.7 28.6 %reduce-scatter.2.cloned.1.call-done = f32[128,256]{1,0:T(8,128)} async-done(((f32[128,1024]{1,0:T(8,128)}), f32[128,256]{1,0:T(8,128)}) %reduce-scatter.2.cloned.1.call-update) | async-done | bytes 131088 | tf_op jit(solution)/shard_map/reduce_scatter | solution.py:49
  275.9 9.7 %all-reduce.3 = (f32[64]{0:T(128)S(1)}, f32[64]{0:T(128)S(1)}, f32[64]{0:T(128)S(1)}) all-reduce(f32[64]{0:T(128)S(1)} %get-tuple-element.9, f32[64]{0:T(128)S(1)} %get-tuple-element.16, f32[64]{0:T(128)S(1)} %get-tuple-element.8), channel_id=1, replica_groups=mesh['blk'=128,'rows'=4] {'rows'}, use_global_device_ids=true, to_apply=%region_4.6 | all-reduce | flops 192 | bytes 1536 | tf_op jit(solution)/shard_map/psum | solution.py:26
  285.7 2.5 multiply_subtract_fusion.3
  290.4 2.8 collective-permute-start.7
  293.2 1.9 collective-permute-start.6
  296.0 7.9 %collective-permute-start.1 = (f32[64,256]{1,0:T(8,128)S(1)}, f32[64,256]{1,0:T(8,128)S(1)}, u32[]{:S(2)}, u32[]{:S(2)}) collective-permute-start(f32[64,256]{1,0:T(8,128)S(1)} %broadcast_select_fusion.7), channel_id=1, source_target_pairs={{0,508},{4,0},{8,4},{12,8},{16,12},{20,16},{24,20},{28,24},{32,28}... | collective-permute-start | bytes 196616 | tf_op jit(solution)/shard_map/ppermute | solution.py:12
  303.9 1.9 collective-permute-start
  307.1 7.2 %collective-permute-done = f32[64,256]{1,0:T(8,128)S(1)} collective-permute-done((f32[64,256]{1,0:T(8,128)S(1)}, f32[64,256]{1,0:T(8,128)S(1)}, u32[]{:S(2)}, u32[]{:S(2)}) %collective-permute-start) | collective-permute-done | bytes 65568 | tf_op jit(solution)/shard_map/ppermute | solution.py:12
  314.5 11.2 %all-reduce.2 = (f32[64]{0:T(128)S(1)}, f32[64]{0:T(128)S(1)}, f32[64]{0:T(128)S(1)}) all-reduce(f32[64]{0:T(128)S(1)} %get-tuple-element.19, f32[64]{0:T(128)S(1)} %get-tuple-element.15, f32[64]{0:T(128)S(1)} %get-tuple-element.14), channel_id=1, replica_groups=mesh['blk'=128,'rows'=4] {'rows'}, use_global_device_ids=true, to_apply=%region_11.13 | all-reduce | flops 192 | bytes 1536 | tf_op jit(solution)/shard_map/psum | solution.py:26
  330.3 1.9 collective-permute-start.9
  332.3 2.4 collective-permute-start.8
  335.5 7.4 %collective-permute-start.3 = (f32[64,256]{1,0:T(8,128)S(1)}, f32[64,256]{1,0:T(8,128)S(1)}, u32[]{:S(2)}, u32[]{:S(2)}) collective-permute-start(f32[64,256]{1,0:T(8,128)S(1)} %broadcast_select_fusion.6), channel_id=1, source_target_pairs={{0,508},{4,0},{8,4},{12,8},{16,12},{20,16},{24,20},{28,24},{32,28}... | collective-permute-start | bytes 196616 | tf_op jit(solution)/shard_map/ppermute | solution.py:12
  342.9 1.9 collective-permute-start.2
  346.1 7.2 %collective-permute-done.2 = f32[64,256]{1,0:T(8,128)S(1)} collective-permute-done((f32[64,256]{1,0:T(8,128)S(1)}, f32[64,256]{1,0:T(8,128)S(1)}, u32[]{:S(2)}, u32[]{:S(2)}) %collective-permute-start.2) | collective-permute-done | bytes 65568 | tf_op jit(solution)/shard_map/ppermute | solution.py:12
  353.6 9.9 %all-reduce.1 = (f32[64]{0:T(128)S(1)}, f32[64]{0:T(128)S(1)}, f32[64]{0:T(128)S(1)}) all-reduce(f32[64]{0:T(128)S(1)} %get-tuple-element.18, f32[64]{0:T(128)S(1)} %get-tuple-element.13, f32[64]{0:T(128)S(1)} %get-tuple-element.12), channel_id=1, replica_groups=mesh['blk'=128,'rows'=4] {'rows'}, use_global_device_ids=true, to_apply=%region_18.20 | all-reduce | flops 192 | bytes 1536 | tf_op jit(solution)/shard_map/psum | solution.py:26
  369.0 1.9 collective-permute-start.11
  370.9 2.4 collective-permute-start.10
  373.4 7.4 %collective-permute-start.5 = (f32[64,256]{1,0:T(8,128)S(1)}, f32[64,256]{1,0:T(8,128)S(1)}, u32[]{:S(2)}, u32[]{:S(2)}) collective-permute-start(f32[64,256]{1,0:T(8,128)S(1)} %broadcast_select_fusion.5), channel_id=1, source_target_pairs={{0,508},{4,0},{8,4},{12,8},{16,12},{20,16},{24,20},{28,24},{32,28}... | collective-permute-start | bytes 196616 | tf_op jit(solution)/shard_map/ppermute | solution.py:12
  380.8 1.9 collective-permute-start.4
  384.8 7.3 %collective-permute-done.4 = f32[64,256]{1,0:T(8,128)S(1)} collective-permute-done((f32[64,256]{1,0:T(8,128)S(1)}, f32[64,256]{1,0:T(8,128)S(1)}, u32[]{:S(2)}, u32[]{:S(2)}) %collective-permute-start.4) | collective-permute-done | bytes 65568 | tf_op jit(solution)/shard_map/ppermute | solution.py:12
  392.2 10.3 %all-reduce = (f32[64]{0:T(128)S(1)}, f32[64]{0:T(128)S(1)}, f32[64]{0:T(128)S(1)}) all-reduce(f32[64]{0:T(128)S(1)} %get-tuple-element.17, f32[64]{0:T(128)S(1)} %get-tuple-element.11, f32[64]{0:T(128)S(1)} %get-tuple-element.10), channel_id=1, replica_groups=mesh['blk'=128,'rows'=4] {'rows'}, use_global_device_ids=true, to_apply=%region_25.27 | all-reduce | flops 192 | bytes 1536 | tf_op jit(solution)/shard_map/psum | solution.py:26
  (93 shorter events, 33.7 us)
Async XLA Ops:
  7.2 3.1 copy-start.3
  7.2 228.3 %all-gather.2.cloned.1.call-start = ((), (), s32[]{:S(2)}) async-start(), calls=%async_computation.1 | async-start | bytes 8454144 | tf_op jit(solution)/shard_map/all_gather | solution.py:45
  7.9 265.4 %reduce-scatter.2.cloned.1.call-start = ((), (), s32[]{:S(2)}) async-start(), calls=%async_computation.2 | async-start | bytes 655360 | tf_op jit(solution)/shard_map/reduce_scatter | solution.py:49
  10.2 225.2 %copy-start = (bf16[4096,128]{1,0:T(8,128)(2,1)S(1)}, bf16[4096,128]{1,0:T(8,128)(2,1)}, u32[]{:S(2)}) copy-start(bf16[4096,128]{1,0:T(8,128)(2,1)} %param.8) | copy-start | bytes 3145732
  289.2 4.0 copy-start.1
  289.2 6.0 %copy-start.2 = (f32[128,256]{1,0:T(8,128)S(1)}, f32[128,256]{1,0:T(8,128)}, u32[]{:S(2)}) copy-start(f32[128,256]{1,0:T(8,128)} %reduce-scatter.2.cloned.1.call-done) | copy-start | bytes 393220
  290.4 35.4 %collective-permute-start.7 = (f32[64,4096]{1,0:T(8,128)}, f32[64,4096]{1,0:T(8,128)S(1)}, u32[]{:S(2)}, u32[]{:S(2)}) collective-permute-start(f32[64,4096]{1,0:T(8,128)} %broadcast_select_fusion.3), channel_id=1, source_target_pairs={{0,508},{4,0},{8,4},{12,8},{16,12},{20,16},{24,20},{28,24},{32,28}... | collective-permute-start | bytes 3145736 | tf_op jit(solution)/shard_map/ppermute | solution.py:12
  293.2 33.5 %collective-permute-start.6 = (f32[64,4096]{1,0:T(8,128)S(1)}, f32[64,4096]{1,0:T(8,128)}, u32[]{:S(2)}, u32[]{:S(2)}) collective-permute-start(f32[64,4096]{1,0:T(8,128)S(1)} %copy-done.1), channel_id=1, source_target_pairs={{0,4},{4,8},{8,12},{12,16},{16,20},{20,24},{24,28},{28,32},{32,36}... | collective-permute-start | bytes 3145736 | tf_op jit(solution)/shard_map/ppermute | solution.py:12
  296.0 10.4 %collective-permute-start.1 = (f32[64,256]{1,0:T(8,128)S(1)}, f32[64,256]{1,0:T(8,128)S(1)}, u32[]{:S(2)}, u32[]{:S(2)}) collective-permute-start(f32[64,256]{1,0:T(8,128)S(1)} %broadcast_select_fusion.7), channel_id=1, source_target_pairs={{0,508},{4,0},{8,4},{12,8},{16,12},{20,16},{24,20},{28,24},{32,28}... | collective-permute-start | bytes 196616 | tf_op jit(solution)/shard_map/ppermute | solution.py:12
  303.9 10.4 %collective-permute-start = (f32[64,256]{1,0:T(8,128)S(1)}, f32[64,256]{1,0:T(8,128)S(1)}, u32[]{:S(2)}, u32[]{:S(2)}) collective-permute-start(f32[64,256]{1,0:T(8,128)S(1)} %get-tuple-element.57), channel_id=1, source_target_pairs={{0,4},{4,8},{8,12},{12,16},{16,20},{20,24},{24,28},{28,32},{32,36}... | collective-permute-start | bytes 196616 | tf_op jit(solution)/shard_map/ppermute | solution.py:12
  330.3 34.1 %collective-permute-start.9 = (f32[64,4096]{1,0:T(8,128)}, f32[64,4096]{1,0:T(8,128)S(1)}, u32[]{:S(2)}, u32[]{:S(2)}) collective-permute-start(f32[64,4096]{1,0:T(8,128)} %broadcast_select_fusion.2), channel_id=1, source_target_pairs={{0,508},{4,0},{8,4},{12,8},{16,12},{20,16},{24,20},{28,24},{32,28}... | collective-permute-start | bytes 3145736 | tf_op jit(solution)/shard_map/ppermute | solution.py:12
  332.3 33.1 %collective-permute-start.8 = (f32[64,4096]{1,0:T(8,128)S(1)}, f32[64,4096]{1,0:T(8,128)}, u32[]{:S(2)}, u32[]{:S(2)}) collective-permute-start(f32[64,4096]{1,0:T(8,128)S(1)} %get-tuple-element.55), channel_id=1, source_target_pairs={{0,4},{4,8},{8,12},{12,16},{16,20},{20,24},{24,28},{28,32},{32,36}... | collective-permute-start | bytes 3145736 | tf_op jit(solution)/shard_map/ppermute | solution.py:12
  335.5 10.0 %collective-permute-start.3 = (f32[64,256]{1,0:T(8,128)S(1)}, f32[64,256]{1,0:T(8,128)S(1)}, u32[]{:S(2)}, u32[]{:S(2)}) collective-permute-start(f32[64,256]{1,0:T(8,128)S(1)} %broadcast_select_fusion.6), channel_id=1, source_target_pairs={{0,508},{4,0},{8,4},{12,8},{16,12},{20,16},{24,20},{28,24},{32,28}... | collective-permute-start | bytes 196616 | tf_op jit(solution)/shard_map/ppermute | solution.py:12
  342.9 10.5 %collective-permute-start.2 = (f32[64,256]{1,0:T(8,128)S(1)}, f32[64,256]{1,0:T(8,128)S(1)}, u32[]{:S(2)}, u32[]{:S(2)}) collective-permute-start(f32[64,256]{1,0:T(8,128)S(1)} %get-tuple-element.63), channel_id=1, source_target_pairs={{0,4},{4,8},{8,12},{12,16},{16,20},{20,24},{24,28},{28,32},{32,36}... | collective-permute-start | bytes 196616 | tf_op jit(solution)/shard_map/ppermute | solution.py:12
  369.0 35.3 %collective-permute-start.11 = (f32[64,4096]{1,0:T(8,128)}, f32[64,4096]{1,0:T(8,128)S(1)}, u32[]{:S(2)}, u32[]{:S(2)}) collective-permute-start(f32[64,4096]{1,0:T(8,128)} %broadcast_select_fusion.1), channel_id=1, source_target_pairs={{0,508},{4,0},{8,4},{12,8},{16,12},{20,16},{24,20},{28,24},{32,28}... | collective-permute-start | bytes 3145736 | tf_op jit(solution)/shard_map/ppermute | solution.py:12
  370.9 34.3 %collective-permute-start.10 = (f32[64,4096]{1,0:T(8,128)S(1)}, f32[64,4096]{1,0:T(8,128)}, u32[]{:S(2)}, u32[]{:S(2)}) collective-permute-start(f32[64,4096]{1,0:T(8,128)S(1)} %get-tuple-element.53), channel_id=1, source_target_pairs={{0,4},{4,8},{8,12},{12,16},{16,20},{20,24},{24,28},{28,32},{32,36}... | collective-permute-start | bytes 3145736 | tf_op jit(solution)/shard_map/ppermute | solution.py:12
  373.4 10.7 %collective-permute-start.5 = (f32[64,256]{1,0:T(8,128)S(1)}, f32[64,256]{1,0:T(8,128)S(1)}, u32[]{:S(2)}, u32[]{:S(2)}) collective-permute-start(f32[64,256]{1,0:T(8,128)S(1)} %broadcast_select_fusion.5), channel_id=1, source_target_pairs={{0,508},{4,0},{8,4},{12,8},{16,12},{20,16},{24,20},{28,24},{32,28}... | collective-permute-start | bytes 196616 | tf_op jit(solution)/shard_map/ppermute | solution.py:12
  380.8 11.3 %collective-permute-start.4 = (f32[64,256]{1,0:T(8,128)S(1)}, f32[64,256]{1,0:T(8,128)S(1)}, u32[]{:S(2)}, u32[]{:S(2)}) collective-permute-start(f32[64,256]{1,0:T(8,128)S(1)} %get-tuple-element.61), channel_id=1, source_target_pairs={{0,4},{4,8},{8,12},{12,16},{16,20},{20,24},{24,28},{28,32},{32,36}... | collective-permute-start | bytes 196616 | tf_op jit(solution)/shard_map/ppermute | solution.py:12
Sparse Core Ops, SparseCore 0:
  10.2 225.2 all-gather.1
  242.8 30.5 reduce-scatter.1
where the time goes:
time: 417 us
  waiting for transfers between devices  277 us (66%)
  starting transfers between devices  41.8 us (10%)
  blocking collectives  41.1 us (10%)
  local copies, waits for them, and re-layouts  19.5 us (5%)
  other arithmetic  15.6 us (4%)
  between operations  14.5 us (3%)
  matrix products  7.14 us (2%)
    all_gather x1, waiting for transfers between devices, per_device(): lax.all_gather(weight, 'blk', axis=0, tiled=True)  223 us
    ppermute x12, starting transfers between devices, shifted(): return lax.ppermute(x, axis, [(i, (i + by) % count) for i in range(count)])  41.7 us
    psum x4, blocking collectives, turn_pair(): lax.psum((upper_norm, lower_norm, cross_term), 'rows')  41.1 us
    reduce_scatter x1, waiting for transfers between devices, per_device(): lax.psum_scatter(partial_cols, 'rows', scatter_dimension=1, tiled=True)  28.6 us
    ppermute x12, waiting for transfers between devices, shifted(): return lax.ppermute(x, axis, [(i, (i + by) % count) for i in range(count)])  24.3 us
  transfers between devices with their start and end apart: 14, of which 8 were waited for; matrix products, arithmetic and copies ran while one was open for 4% of the time, Pallas kernels for 0%

commit v1 on v0

--- a/solution.py
+++ b/solution.py
@@ -42,7 +42,9 @@
 def per_device(weight, factor, pairing):
     partial_cols = lax.dot_general(
         factor,
-        lax.all_gather(weight, "blk", axis=0, tiled=True),
+        jnp.concatenate(
+            lax.all_to_all(jnp.stack([weight] * lax.axis_size("blk")), "blk", 0, 0), axis=0
+        ),
         (((0,), (1,)), ((), ())),
         preferred_element_type=jnp.float32,
     )

time: 417 us -> 394 us (0.945)
  waiting for transfers between devices: 277 us -> 224 us
  starting transfers between devices: 41.8 us -> 67.7 us
    all_gather x1 -> x0, waiting for transfers between devices: 223 us -> none  [per_device(): lax.all_gather(weight, 'blk', axis=0, tiled=True)]
    all_to_all x0 -> x1, waiting for transfers between devices: none -> 183 us  [per_device(): lax.all_to_all(jnp.stack([weight] * lax.axis_size('blk')), 'blk', 0, 0)]
    all_to_all x0 -> x1, starting transfers between devices: none -> 14.3 us  [per_device(): lax.all_to_all(jnp.stack([weight] * lax.axis_size('blk')), 'blk', 0, 0)]
    ppermute x12, starting transfers between devices: 41.7 us -> 53.3 us  [shifted(): return lax.ppermute(x, axis, [(i, (i + by) % count) for i in range(count)])]
    ppermute x12, waiting for transfers between devices: 24.3 us -> 15.2 us  [shifted(): return lax.ppermute(x, axis, [(i, (i + by) % count) for i in range(count)])]
    another operation x0 -> x1, local copies, waits for them, and re-layouts: none -> 5.09 us  [per_device(): jnp.stack([weight] * lax.axis_size('blk'))]
  transfers between devices with their start and end apart: 14 -> 14, of which waited for: 8 -> 5; matrix products, arithmetic and copies ran while one was open for 4% -> 5% of each run, Pallas kernels for 0% -> 0%
where the time goes in v1:
time: 394 us; the launch traced here: 393 us
  waiting for transfers between devices  224 us (57%)
  starting transfers between devices  67.7 us (17%)
  blocking collectives  41.6 us (11%)
  local copies, waits for them, and re-layouts  23.6 us (6%)
  between operations  14.6 us (4%)
  other arithmetic  14.3 us (4%)
  matrix products  7.14 us (2%)
    all_to_all x1, waiting for transfers between devices, per_device(): lax.all_to_all(jnp.stack([weight] * lax.axis_size('blk')), 'blk', 0, 0)  183 us
    ppermute x12, starting transfers between devices, shifted(): return lax.ppermute(x, axis, [(i, (i + by) % count) for i in range(count)])  53.3 us
    psum x4, blocking collectives, turn_pair(): lax.psum((upper_norm, lower_norm, cross_term), 'rows')  41.6 us
    reduce_scatter x1, waiting for transfers between devices, per_device(): lax.psum_scatter(partial_cols, 'rows', scatter_dimension=1, tiled=True)  26.2 us
    ppermute x12, waiting for transfers between devices, shifted(): return lax.ppermute(x, axis, [(i, (i + by) % count) for i in range(count)])  15.2 us
    all_to_all x1, starting transfers between devices, per_device(): lax.all_to_all(jnp.stack([weight] * lax.axis_size('blk')), 'blk', 0, 0)  14.3 us
  transfers between devices with their start and end apart: 14, of which 5 were waited for; matrix products, arithmetic and copies ran while one was open for 5% of the time, Pallas kernels for 0%

profile of v1, /device:TPU:128, one launch (start us, length us, event | category | flops | bytes accessed | tf_op | source)
XLA Modules:
  0.0 393.3 jit_solution(16112007846726537673)
XLA Ops:
  7.2 5.1 %stack.2 = bf16[128,8,4096]{2,1,0:T(8,128)(2,1)} broadcast(bf16[8,4096]{1,0:T(8,128)(2,1)} %param.7), dimensions={1,2} | broadcast | bytes 8454144 | tf_op jit(solution)/shard_map/stack | solution.py:46
  12.3 14.3 %all-to-all-start = ((bf16[128,8,4096]{2,1,0:T(8,128)(2,1)}), bf16[128,8,4096]{2,1,0:T(8,128)(2,1)}, u32[]{:S(2)}, u32[]{:S(2)}) async-start(bf16[128,8,4096]{2,1,0:T(8,128)(2,1)} %stack.2), calls=%async_computation | async-start | bytes 16777216 | tf_op jit(solution)/shard_map/all_to_all | solution.py:46
  29.7 183.0 %all-to-all-done = bf16[128,8,4096]{2,1,0:T(8,128)(2,1)} async-done(((bf16[128,8,4096]{2,1,0:T(8,128)(2,1)}), bf16[128,8,4096]{2,1,0:T(8,128)(2,1)}, u32[]{:S(2)}, u32[]{:S(2)}) %all-to-all-start) | async-done | bytes 8388640 | tf_op jit(solution)/shard_map/all_to_all | solution.py:46
  212.7 7.1 %fusion = f32[128,1024]{1,0:T(8,128)} fusion(bf16[4096,128]{1,0:T(8,128)(2,1)S(1)} %copy-done, bf16[128,8,4096]{2,1,0:T(8,128)(2,1)} %all-to-all-done), kind=kOutput, calls=%fused_computation.16 | convolution fusion | flops 1073741824 | bytes 9961472 | tf_op jit(solution)/shard_map/dot_general | solution.py:43
  221.9 26.2 %reduce-scatter.2.cloned.1.call-done = f32[128,256]{1,0:T(8,128)} async-done(((f32[128,1024]{1,0:T(8,128)}), f32[128,256]{1,0:T(8,128)}) %reduce-scatter.2.cloned.1.call-update) | async-done | bytes 131088 | tf_op jit(solution)/shard_map/reduce_scatter | solution.py:51
  250.7 9.6 %all-reduce.3 = (f32[64]{0:T(128)S(1)}, f32[64]{0:T(128)S(1)}, f32[64]{0:T(128)S(1)}) all-reduce(f32[64]{0:T(128)S(1)} %get-tuple-element.9, f32[64]{0:T(128)S(1)} %get-tuple-element.16, f32[64]{0:T(128)S(1)} %get-tuple-element.8), channel_id=1, replica_groups=mesh['blk'=128,'rows'=4] {'rows'}, use_global_device_ids=true, to_apply=%region_4.6 | all-reduce | flops 192 | bytes 1536 | tf_op jit(solution)/shard_map/psum | solution.py:26
  260.4 2.5 multiply_subtract_fusion.3
  262.9 1.9 collective-permute-start.6
  266.0 7.9 %collective-permute-start.7 = (f32[64,4096]{1,0:T(8,128)S(1)}, f32[64,4096]{1,0:T(8,128)S(1)}, u32[]{:S(2)}, u32[]{:S(2)}) collective-permute-start(f32[64,4096]{1,0:T(8,128)S(1)} %broadcast_select_fusion.3), channel_id=1, source_target_pairs={{0,508},{4,0},{8,4},{12,8},{16,12},{20,16},{24,20},{28,24},{32,28}... | collective-permute-start | bytes 3145736 | tf_op jit(solution)/shard_map/ppermute | solution.py:12
  274.0 1.9 collective-permute-start
  276.6 7.9 %collective-permute-start.1 = (f32[64,256]{1,0:T(8,128)S(1)}, f32[64,256]{1,0:T(8,128)S(1)}, u32[]{:S(2)}, u32[]{:S(2)}) collective-permute-start(f32[64,256]{1,0:T(8,128)S(1)} %broadcast_select_fusion.7), channel_id=1, source_target_pairs={{0,508},{4,0},{8,4},{12,8},{16,12},{20,16},{24,20},{28,24},{32,28}... | collective-permute-start | bytes 196616 | tf_op jit(solution)/shard_map/ppermute | solution.py:12
  284.5 2.3 collective-permute-done.1
  287.7 11.6 %all-reduce.2 = (f32[64]{0:T(128)S(1)}, f32[64]{0:T(128)S(1)}, f32[64]{0:T(128)S(1)}) all-reduce(f32[64]{0:T(128)S(1)} %get-tuple-element.19, f32[64]{0:T(128)S(1)} %get-tuple-element.15, f32[64]{0:T(128)S(1)} %get-tuple-element.14), channel_id=1, replica_groups=mesh['blk'=128,'rows'=4] {'rows'}, use_global_device_ids=true, to_apply=%region_11.13 | all-reduce | flops 192 | bytes 1536 | tf_op jit(solution)/shard_map/psum | solution.py:26
  300.4 2.5 multiply_subtract_fusion.2
  306.9 7.8 %collective-permute-start.9 = (f32[64,4096]{1,0:T(8,128)}, f32[64,4096]{1,0:T(8,128)S(1)}, u32[]{:S(2)}, u32[]{:S(2)}) collective-permute-start(f32[64,4096]{1,0:T(8,128)} %broadcast_select_fusion.2), channel_id=1, source_target_pairs={{0,508},{4,0},{8,4},{12,8},{16,12},{20,16},{24,20},{28,24},{32,28}... | collective-permute-start | bytes 3145736 | tf_op jit(solution)/shard_map/ppermute | solution.py:12
  314.9 1.9 collective-permute-start.2
  317.6 7.9 %collective-permute-start.3 = (f32[64,256]{1,0:T(8,128)S(1)}, f32[64,256]{1,0:T(8,128)S(1)}, u32[]{:S(2)}, u32[]{:S(2)}) collective-permute-start(f32[64,256]{1,0:T(8,128)S(1)} %broadcast_select_fusion.6), channel_id=1, source_target_pairs={{0,508},{4,0},{8,4},{12,8},{16,12},{20,16},{24,20},{28,24},{32,28}... | collective-permute-start | bytes 196616 | tf_op jit(solution)/shard_map/ppermute | solution.py:12
  325.4 2.6 collective-permute-done.3
  328.9 8.6 %all-reduce.1 = (f32[64]{0:T(128)S(1)}, f32[64]{0:T(128)S(1)}, f32[64]{0:T(128)S(1)}) all-reduce(f32[64]{0:T(128)S(1)} %get-tuple-element.18, f32[64]{0:T(128)S(1)} %get-tuple-element.13, f32[64]{0:T(128)S(1)} %get-tuple-element.12), channel_id=1, replica_groups=mesh['blk'=128,'rows'=4] {'rows'}, use_global_device_ids=true, to_apply=%region_18.20 | all-reduce | flops 192 | bytes 1536 | tf_op jit(solution)/shard_map/psum | solution.py:26
  337.8 1.9 collective-permute-start.4
  345.6 8.0 %collective-permute-start.11 = (f32[64,4096]{1,0:T(8,128)S(1)}, f32[64,4096]{1,0:T(8,128)S(1)}, u32[]{:S(2)}, u32[]{:S(2)}) collective-permute-start(f32[64,4096]{1,0:T(8,128)S(1)} %broadcast_select_fusion.1), channel_id=1, source_target_pairs={{0,508},{4,0},{8,4},{12,8},{16,12},{20,16},{24,20},{28,24},{32,28}... | collective-permute-start | bytes 3145736 | tf_op jit(solution)/shard_map/ppermute | solution.py:12
  353.7 2.4 collective-permute-start.5
  356.2 10.3 %collective-permute-done.5 = f32[64,256]{1,0:T(8,128)S(1)} collective-permute-done((f32[64,256]{1,0:T(8,128)S(1)}, f32[64,256]{1,0:T(8,128)S(1)}, u32[]{:S(2)}, u32[]{:S(2)}) %collective-permute-start.5) | collective-permute-done | bytes 65568 | tf_op jit(solution)/shard_map/ppermute | solution.py:12
  367.4 11.8 %all-reduce = (f32[64]{0:T(128)S(1)}, f32[64]{0:T(128)S(1)}, f32[64]{0:T(128)S(1)}) all-reduce(f32[64]{0:T(128)S(1)} %get-tuple-element.17, f32[64]{0:T(128)S(1)} %get-tuple-element.11, f32[64]{0:T(128)S(1)} %get-tuple-element.10), channel_id=1, replica_groups=mesh['blk'=128,'rows'=4] {'rows'}, use_global_device_ids=true, to_apply=%region_25.27 | all-reduce | flops 192 | bytes 1536 | tf_op jit(solution)/shard_map/psum | solution.py:26
  (91 shorter events, 31.6 us)
Async XLA Ops:
  12.3 14.3 %copy-start = (bf16[4096,128]{1,0:T(8,128)(2,1)S(1)}, bf16[4096,128]{1,0:T(8,128)(2,1)}, u32[]{:S(2)}) copy-start(bf16[4096,128]{1,0:T(8,128)(2,1)} %param.8) | copy-start | bytes 3145732
  12.3 200.4 %all-to-all-start = ((bf16[128,8,4096]{2,1,0:T(8,128)(2,1)}), bf16[128,8,4096]{2,1,0:T(8,128)(2,1)}, u32[]{:S(2)}, u32[]{:S(2)}) async-start(bf16[128,8,4096]{2,1,0:T(8,128)(2,1)} %stack.2), calls=%async_computation | async-start | bytes 16777216 | tf_op jit(solution)/shard_map/all_to_all | solution.py:46
  26.5 1.4 copy-start.2
  26.5 221.6 %reduce-scatter.2.cloned.1.call-start = ((), (), s32[]{:S(2)}) async-start(), calls=%async_computation.2 | async-start | bytes 655360 | tf_op jit(solution)/shard_map/reduce_scatter | solution.py:51
  262.9 37.4 %collective-permute-start.6 = (f32[64,4096]{1,0:T(8,128)}, f32[64,4096]{1,0:T(8,128)}, u32[]{:S(2)}, u32[]{:S(2)}) collective-permute-start(f32[64,4096]{1,0:T(8,128)} %get-tuple-element.49), channel_id=1, source_target_pairs={{0,4},{4,8},{8,12},{12,16},{16,20},{20,24},{24,28},{28,32},{32,36}... | collective-permute-start | bytes 3145736 | tf_op jit(solution)/shard_map/ppermute | solution.py:12
  265.8 8.1 %copy-start.1 = (f32[128,256]{1,0:T(8,128)S(1)}, f32[128,256]{1,0:T(8,128)}, u32[]{:S(2)}) copy-start(f32[128,256]{1,0:T(8,128)} %reduce-scatter.2.cloned.1.call-done) | copy-start | bytes 393220
  266.0 33.5 %collective-permute-start.7 = (f32[64,4096]{1,0:T(8,128)S(1)}, f32[64,4096]{1,0:T(8,128)S(1)}, u32[]{:S(2)}, u32[]{:S(2)}) collective-permute-start(f32[64,4096]{1,0:T(8,128)S(1)} %broadcast_select_fusion.3), channel_id=1, source_target_pairs={{0,508},{4,0},{8,4},{12,8},{16,12},{20,16},{24,20},{28,24},{32,28}... | collective-permute-start | bytes 3145736 | tf_op jit(solution)/shard_map/ppermute | solution.py:12
  274.0 13.5 %collective-permute-start = (f32[64,256]{1,0:T(8,128)S(1)}, f32[64,256]{1,0:T(8,128)S(1)}, u32[]{:S(2)}, u32[]{:S(2)}) collective-permute-start(f32[64,256]{1,0:T(8,128)S(1)} %get-tuple-element.57), channel_id=1, source_target_pairs={{0,4},{4,8},{8,12},{12,16},{16,20},{20,24},{24,28},{28,32},{32,36}... | collective-permute-start | bytes 196616 | tf_op jit(solution)/shard_map/ppermute | solution.py:12
  276.6 10.2 %collective-permute-start.1 = (f32[64,256]{1,0:T(8,128)S(1)}, f32[64,256]{1,0:T(8,128)S(1)}, u32[]{:S(2)}, u32[]{:S(2)}) collective-permute-start(f32[64,256]{1,0:T(8,128)S(1)} %broadcast_select_fusion.7), channel_id=1, source_target_pairs={{0,508},{4,0},{8,4},{12,8},{16,12},{20,16},{24,20},{28,24},{32,28}... | collective-permute-start | bytes 196616 | tf_op jit(solution)/shard_map/ppermute | solution.py:12
  302.9 38.3 %collective-permute-start.8 = (f32[64,4096]{1,0:T(8,128)}, f32[64,4096]{1,0:T(8,128)S(1)}, u32[]{:S(2)}, u32[]{:S(2)}) collective-permute-start(f32[64,4096]{1,0:T(8,128)} %get-tuple-element.55), channel_id=1, source_target_pairs={{0,4},{4,8},{8,12},{12,16},{16,20},{20,24},{24,28},{28,32},{32,36}... | collective-permute-start | bytes 3145736 | tf_op jit(solution)/shard_map/ppermute | solution.py:12
  306.9 33.4 %collective-permute-start.9 = (f32[64,4096]{1,0:T(8,128)}, f32[64,4096]{1,0:T(8,128)S(1)}, u32[]{:S(2)}, u32[]{:S(2)}) collective-permute-start(f32[64,4096]{1,0:T(8,128)} %broadcast_select_fusion.2), channel_id=1, source_target_pairs={{0,508},{4,0},{8,4},{12,8},{16,12},{20,16},{24,20},{28,24},{32,28}... | collective-permute-start | bytes 3145736 | tf_op jit(solution)/shard_map/ppermute | solution.py:12
  314.9 13.8 %collective-permute-start.2 = (f32[64,256]{1,0:T(8,128)S(1)}, f32[64,256]{1,0:T(8,128)S(1)}, u32[]{:S(2)}, u32[]{:S(2)}) collective-permute-start(f32[64,256]{1,0:T(8,128)S(1)} %get-tuple-element.63), channel_id=1, source_target_pairs={{0,4},{4,8},{8,12},{12,16},{16,20},{20,24},{24,28},{28,32},{32,36}... | collective-permute-start | bytes 196616 | tf_op jit(solution)/shard_map/ppermute | solution.py:12
  317.6 10.4 %collective-permute-start.3 = (f32[64,256]{1,0:T(8,128)S(1)}, f32[64,256]{1,0:T(8,128)S(1)}, u32[]{:S(2)}, u32[]{:S(2)}) collective-permute-start(f32[64,256]{1,0:T(8,128)S(1)} %broadcast_select_fusion.6), channel_id=1, source_target_pairs={{0,508},{4,0},{8,4},{12,8},{16,12},{20,16},{24,20},{28,24},{32,28}... | collective-permute-start | bytes 196616 | tf_op jit(solution)/shard_map/ppermute | solution.py:12
  337.8 29.4 %collective-permute-start.4 = (f32[64,256]{1,0:T(8,128)S(1)}, f32[64,256]{1,0:T(8,128)S(1)}, u32[]{:S(2)}, u32[]{:S(2)}) collective-permute-start(f32[64,256]{1,0:T(8,128)S(1)} %get-tuple-element.61), channel_id=1, source_target_pairs={{0,4},{4,8},{8,12},{12,16},{16,20},{20,24},{24,28},{28,32},{32,36}... | collective-permute-start | bytes 196616 | tf_op jit(solution)/shard_map/ppermute | solution.py:12
  342.6 39.2 %collective-permute-start.10 = (f32[64,4096]{1,0:T(8,128)}, f32[64,4096]{1,0:T(8,128)}, u32[]{:S(2)}, u32[]{:S(2)}) collective-permute-start(f32[64,4096]{1,0:T(8,128)} %get-tuple-element.53), channel_id=1, source_target_pairs={{0,4},{4,8},{8,12},{12,16},{16,20},{20,24},{24,28},{28,32},{32,36}... | collective-permute-start | bytes 3145736 | tf_op jit(solution)/shard_map/ppermute | solution.py:12
  345.6 35.3 %collective-permute-start.11 = (f32[64,4096]{1,0:T(8,128)S(1)}, f32[64,4096]{1,0:T(8,128)S(1)}, u32[]{:S(2)}, u32[]{:S(2)}) collective-permute-start(f32[64,4096]{1,0:T(8,128)S(1)} %broadcast_select_fusion.1), channel_id=1, source_target_pairs={{0,508},{4,0},{8,4},{12,8},{16,12},{20,16},{24,20},{28,24},{32,28}... | collective-permute-start | bytes 3145736 | tf_op jit(solution)/shard_map/ppermute | solution.py:12
  353.7 12.7 %collective-permute-start.5 = (f32[64,256]{1,0:T(8,128)S(1)}, f32[64,256]{1,0:T(8,128)S(1)}, u32[]{:S(2)}, u32[]{:S(2)}) collective-permute-start(f32[64,256]{1,0:T(8,128)S(1)} %broadcast_select_fusion.5), channel_id=1, source_target_pairs={{0,508},{4,0},{8,4},{12,8},{16,12},{20,16},{24,20},{28,24},{32,28}... | collective-permute-start | bytes 196616 | tf_op jit(solution)/shard_map/ppermute | solution.py:12
Sparse Core Ops, SparseCore 0:
  220.0 28.1 reduce-scatter.1
